TPU v7x, 32 devices: a whole 2x2x4 slice. The times are simulated.
32 devices in a mesh: dp: 1, expert: 32 (over z, y, x, core).
Axes of the slice: x: 2, y: 2, z: 4, core: 2. Of those that a mesh axis runs over, the one named last changes fastest.
Arguments:
- queries: bfloat16 [1024, 4096], P('dp', 'expert'), may hold values from -140 to 140
- keys: bfloat16 [1024, 256], P(('dp', 'expert')), may hold values from -4 to 4
- values: bfloat16 [1024, 256], P(('dp', 'expert')), may hold values from -4 to 4
- span_ids: int32 [1024], P('dp'), may hold values from 0 to 9, as said below
- residual: bfloat16 [1024, 4096], P(('dp', 'expert')), may hold values from -6 to 6
- norm_gain: float32 [4096], replicated, may hold values from 0.1 to 1.9
- routes: int32 [1024, 8], P(('dp', 'expert')), may hold values from 0 to 127, as said below
- gates: float32 [1024, 8], P(('dp', 'expert')), may hold values from 0.2 to 1
- w_gate: bfloat16 [4096, 4096], P('expert'), may hold values from -0.09375 to 0.09375
- w_up: bfloat16 [4096, 4096], P('expert'), may hold values from -0.09375 to 0.09375
- w_down: bfloat16 [4096, 4096], P('expert'), may hold values from -0.1875 to 0.1875
Outputs:
- mixed: bfloat16 [1024, 4096], P(('dp', 'expert'))
Inputs may be any that keep to these rules, and one draw needn't show every extreme that they name: `span_ids`: span numbers start at 0 and never fall along the positions; every span starts at an even position, has 2 to 512 positions and never crosses a multiple of 512; one aligned block of 512 positions is a single span, and every other holds exactly 9 spans. `routes`: each row names 8 different experts. In the rows of one device (aligned blocks of 32 rows) each expert below 4 is named by at most 8 rows, and exactly one such expert, changing from block to block, by exactly 8 rows; every expert below 4 is that one in some block.
All inputs are finite; a program needn't handle non-finite values.
Results may differ from a plain program's by a relative error of at most 0.0054.
Values may be sent and summed in bfloat16 or wider, within the bound.
A program may use at most 64 MiB of HBM per device.

v0:
```python
import functools
import math

import jax
import jax.numpy as jnp
from jax import lax
from jax.experimental import pallas as pl
from jax.experimental.pallas import tpu as pltpu
from jax.sharding import PartitionSpec as P

KV_HEADS = 4
HEAD_DIM = 64
FF_WIN = 1024
SPAN = 512
MESH = pl.DeviceIdType.MESH
F32 = jnp.float32
BF16 = jnp.bfloat16


def remote(src, dst, send, recv, device):
    return pltpu.make_async_remote_copy(
        src_ref=src, dst_ref=dst, send_sem=send, recv_sem=recv,
        device_id={"expert": device}, device_id_type=MESH,
    )


def route_matrix(routes, gates, wave, capacity):
    tokens = routes.shape[0]
    columns = wave * capacity
    column = lax.broadcasted_iota(jnp.int32, (tokens, columns), 1)
    lower = (
        lax.broadcasted_iota(jnp.int32, (tokens, tokens), 0)
        >= lax.broadcasted_iota(jnp.int32, (tokens, tokens), 1)
    ).astype(F32)
    named_wide = jnp.zeros((tokens, columns), F32)
    weight_wide = jnp.zeros((tokens, columns), F32)
    for expert in range(wave):
        hits = routes == expert
        named = jnp.max(jnp.where(hits, 1.0, 0.0), axis=1, keepdims=True)
        weight = jnp.sum(jnp.where(hits, gates, 0.0), axis=1, keepdims=True)
        here = column // capacity == expert
        named_wide = jnp.where(here, named, named_wide)
        weight_wide = jnp.where(here, weight, weight_wide)
    count = jnp.dot(lower.astype(BF16), named_wide.astype(BF16), preferred_element_type=F32)
    slot = (column % capacity + 1).astype(F32)
    chosen = jnp.where(count == slot, named_wide, 0.0)
    return chosen, chosen * weight_wide


def moe_kernel(
    group, queries_hbm, keys_hbm, values_hbm, ids_hbm, res_hbm, gain_hbm, routes_hbm, gates_hbm, wg, wu, wd, out,
    queries, keys, values, ids, res, gain, routes, gates, in_sem,
    kv_out, kv_buf, id_rows, att_in, att_own, att_buf,
    kz_send, kv_send, kv_recv, az_send, az_recv, a_send, a_recv,
    wgu_v, wd_v, outg, x_buf, part, core_buf, sums, plane_buf, final, back,
    w_sem, z_send, x_send, x_recv, c_send, c_recv, p_send, p_recv, b_send, b_recv,
):
    me = lax.axis_index("expert")
    wave = outg.shape[0]
    capacity = outg.shape[1] // 2
    tokens, width = out.shape
    half = width // 2
    hidden_here = wg.shape[0]
    mine = me % group
    plane = me // group
    base = plane * group

    def across(rz):
        return (plane ^ rz) * group + mine

    def within(r):
        return base + (mine ^ r)

    fetched = {}
    for number, (name, source, target) in enumerate((
        ("keys", keys_hbm, keys), ("values", values_hbm, values), ("ids", ids_hbm, ids),
        ("routes", routes_hbm, routes), ("gates", gates_hbm, gates), ("queries", queries_hbm, queries),
        ("res", res_hbm, res), ("gain", gain_hbm, gain),
    )):
        fetched[name] = pltpu.make_async_copy(source, target, in_sem.at[number])
    weights = [
        pltpu.make_async_copy(wg, wgu_v.at[pl.ds(0, hidden_here)], w_sem.at[0]),
        pltpu.make_async_copy(wu, wgu_v.at[pl.ds(hidden_here, hidden_here)], w_sem.at[1]),
        pltpu.make_async_copy(wd, wd_v, w_sem.at[2]),
    ]
    barrier = pltpu.get_barrier_semaphore()
    partners = [across(rz) for rz in range(1, wave)] + [within(r) for r in range(1, group)]
    for device in partners:
        pl.semaphore_signal(barrier, inc=1, device_id={"expert": device}, device_id_type=MESH)

    for copy in list(fetched.values()) + weights:
        copy.start()
    for name in ("keys", "values"):
        fetched[name].wait()
    for plane_to in range(wave):
        head = plane_to * KV_HEADS // wave
        columns = slice(head * HEAD_DIM, (head + 1) * HEAD_DIM)
        kv_out[plane_to] = jnp.concatenate([keys[:, columns], values[:, columns]], axis=1)
    pl.semaphore_wait(barrier, len(partners))

    sends = []

    def go(copy):
        copy.start()
        sends.append(copy)
        return copy

    def arrived(ref, sem):
        pltpu.make_async_copy(ref, ref, sem).wait()

    for rz in range(1, wave):
        go(remote(kv_out.at[plane ^ rz], kv_buf.at[plane, mine], kz_send.at[rz], kv_recv.at[rz, 0], across(rz)))
    kv_buf[plane, mine] = kv_out[plane]
    for rz in range(wave):
        block = kv_buf.at[plane ^ rz, mine]
        if rz:
            arrived(block, kv_recv.at[rz, 0])
    for r in range(1, group):
        block = kv_buf.at[:, mine]
        go(remote(block, block, kv_send.at[0, r], kv_recv.at[0, r], within(r)))

    for name in ("ids", "routes", "gates", "queries"):
        fetched[name].wait()
    chosen, mix = route_matrix(routes[...].astype(F32).T, gates[...].T, wave, capacity)
    chunk = group * tokens
    for index in range(wave):
        id_rows[index] = jnp.broadcast_to(ids[index].astype(F32), (128, chunk)).T
    for r in range(1, group):
        arrived(kv_buf.at[:, mine ^ r], kv_recv.at[0, r])

    def attend(index):
        planes = SPAN // chunk
        first = index // planes * planes
        block = kv_buf[pl.ds(first, planes)].reshape(SPAN, 2 * HEAD_DIM)
        key_blk = block[:, :HEAD_DIM]
        value_rows = block.T[HEAD_DIM:]
        key_ids = id_rows[pl.ds(first, planes)].reshape(SPAN, 128)
        key_ids = jnp.concatenate([key_ids] * (chunk // 128), axis=1)
        offset = (index - first) * chunk
        ahead = (
            lax.broadcasted_iota(jnp.int32, (SPAN, chunk), 0)
            - lax.broadcasted_iota(jnp.int32, (SPAN, chunk), 1)
        )
        allowed = (ahead <= offset) & (key_ids == ids[index].astype(F32))
        query = queries[pl.ds(pl.multiple_of(index * chunk, chunk), chunk), :] * BF16(1.0 / math.sqrt(HEAD_DIM))
        heads = []
        for head in range(query.shape[1] // HEAD_DIM):
            one = query[:, head * HEAD_DIM:(head + 1) * HEAD_DIM]
            scores = lax.dot_general(key_blk, one, (((1,), (1,)), ((), ())), preferred_element_type=F32)
            scores = jnp.where(allowed, scores, -jnp.inf)
            raised = jnp.exp(scores - jnp.max(scores, axis=0, keepdims=True))
            weights_here = raised * (1.0 / jnp.sum(raised, axis=0, keepdims=True))
            heads.append(jnp.dot(value_rows, weights_here.astype(BF16), preferred_element_type=F32))
        joined = heads[0] if len(heads) == 1 else jnp.concatenate(heads, axis=0)
        return joined.T.astype(BF16).reshape(group, tokens, query.shape[1])

    later = wave // 2

    def spread(part_at, first):
        block = pl.ds(first, later)
        for rz in range(first, first + later):
            if rz:
                arrived(att_in.at[rz], az_recv.at[rz])
        for r in range(1, group):
            go(remote(att_in.at[block, mine ^ r], att_buf.at[block, mine],
                      a_send.at[part_at, r], a_recv.at[part_at, r], within(r)))
        att_buf[block, mine] = att_in[block, mine]

    for rz in range(wave - 1, 0, -1):
        att_own[rz] = attend(plane ^ rz)
        go(remote(att_own.at[rz], att_in.at[rz], az_send.at[rz], az_recv.at[rz], across(rz)))
    spread(0, later)
    att_in[0] = attend(plane)
    spread(1, 0)
    for part_at, first in ((0, later), (1, 0)):
        for r in range(1, group):
            arrived(att_buf.at[pl.ds(first, later), mine ^ r], a_recv.at[part_at, r])
    att = jnp.concatenate(
        [att_buf[plane ^ (index // group), index % group] for index in range(wave * group)], axis=1
    )
    for name in ("res", "gain"):
        fetched[name].wait()
    stream = (res[...].astype(F32) + att.astype(F32)).astype(BF16).astype(F32)
    inverse = lax.rsqrt(jnp.mean(stream * stream, axis=-1, keepdims=True) + 1e-06)
    normed = (stream * inverse * gain[...]).astype(BF16)
    rows = jnp.dot(chosen.T.astype(BF16), normed, preferred_element_type=F32)
    for expert in range(wave):
        block = rows[expert * capacity:(expert + 1) * capacity]
        outg[expert] = jnp.concatenate([block[:, :half], block[:, half:]], axis=0).astype(BF16)
    for rz in range(1, wave):
        go(remote(outg.at[plane ^ rz], x_buf.at[0, rz], z_send.at[rz], x_recv.at[0, rz], across(rz)))
    x_buf[0, 0] = outg[plane]
    for rz in range(wave):
        if rz:
            arrived(x_buf.at[0, rz], x_recv.at[0, rz])
        for r in (2, 4, 1):
            go(remote(x_buf.at[0, rz], x_buf.at[r, rz], x_send.at[r, rz], x_recv.at[r, rz], within(r)))
    for copy in weights:
        copy.wait()

    def fold(k):
        arrived(core_buf.at[k], c_recv.at[k])
        for rz in range(wave - 1, -1, -1):
            sums[k, rz] = (part[2 * k, rz].astype(F32) + core_buf[k, rz].astype(F32)).astype(BF16)
            go(remote(sums.at[k, rz], plane_buf.at[k, rz], p_send.at[k, rz], p_recv.at[k, rz], within(2 * k)))

    def landed(r, rz):
        arrived(x_buf.at[r, rz], x_recv.at[r, rz])
        go(remote(x_buf.at[r, rz], x_buf.at[r + 1, rz], x_send.at[r + 1, rz], x_recv.at[r + 1, rz], within(1)))

    dims = (((1,), (1,)), ((), ()))
    pairs = group // 2
    for k in range(pairs):
        r = 2 * k
        if k == 1:
            for rz in range(wave):
                for near, other in ((2, 4), (4, 2)):
                    landed(near, rz)
                    if (rz < wave // 2) == (near == 4):
                        go(remote(x_buf.at[near, rz], x_buf.at[6, rz], x_send.at[6, rz],
                                  x_recv.at[6, rz], within(other)))
        if k == 3:
            for rz in range(wave):
                landed(6, rz)
        for rz in range(wave):
            arrived(x_buf.at[r + 1, rz], x_recv.at[r + 1, rz])
        x = x_buf[r:r + 2].reshape(2 * wave * 2 * capacity, half)
        left = lax.dot_general(x, wgu_v[:, :half], dims, preferred_element_type=F32)
        right = lax.dot_general(x, wgu_v[:, half:], dims, preferred_element_type=F32)
        left = left.reshape(2 * wave, 2 * capacity, 2 * hidden_here)[:, :capacity]
        right = right.reshape(2 * wave, 2 * capacity, 2 * hidden_here)[:, capacity:]
        pre = (left + right).reshape(2 * wave * capacity, 2 * hidden_here)
        gate_pre, up_pre = pre[:, :hidden_here], pre[:, hidden_here:]
        hidden = (gate_pre / (1.0 + jnp.exp(-gate_pre)) * up_pre).astype(BF16)
        piece = jnp.dot(hidden, wd_v[...], preferred_element_type=F32)
        for number in range(2 * wave):
            block = piece[number * capacity:(number + 1) * capacity]
            block = jnp.concatenate([block[:, :half], block[:, half:]], axis=0).astype(BF16)
            part[r + number // wave, number % wave] = block
        go(remote(part.at[r + 1], core_buf.at[k], c_send.at[k], c_recv.at[k], within(1)))
        if k > 1:
            fold(k - 1)
    fold(pairs - 1)

    arrived(core_buf.at[0], c_recv.at[0])
    for rz in range(wave - 1, -1, -1):
        total = part[0, rz].astype(F32) + core_buf[0, rz].astype(F32)
        for k in range(1, pairs):
            arrived(plane_buf.at[k, rz], p_recv.at[k, rz])
            total = total + plane_buf[k, rz].astype(F32)
        if rz:
            final[rz] = total.astype(BF16)
            go(remote(final.at[rz], back.at[plane], b_send.at[rz], b_recv.at[rz], across(rz)))
        else:
            back[plane] = total.astype(BF16)
    for rz in range(1, wave):
        arrived(back.at[plane ^ rz], b_recv.at[rz])

    high = mix.astype(BF16)
    rest = mix - high.astype(F32)
    middle = rest.astype(BF16)
    low = (rest - middle.astype(F32)).astype(BF16)
    outs = back[...].astype(F32)
    for side in range(2):
        columns = slice(side * half, (side + 1) * half)
        block = outs[:, side * capacity:(side + 1) * capacity].reshape(wave * capacity, half).astype(BF16)
        added = (
            jnp.dot(low, block, preferred_element_type=F32)
            + jnp.dot(middle, block, preferred_element_type=F32)
            + jnp.dot(high, block, preferred_element_type=F32)
        )
        out[:, columns] = (stream[:, columns] + added).astype(BF16)
    for copy in sends:
        copy.wait_send()


def layer(queries, keys, values, span_ids, res, gain, routes, gates, wg, wu, wd):
    devices = lax.axis_size("expert")
    group = FF_WIN // wg.shape[0]
    wave = devices // group
    tokens, width = res.shape
    capacity = tokens // 4
    half = width // 2
    pairs = group // 2
    vmem = pl.BlockSpec(memory_space=pltpu.VMEM)
    hbm = pl.BlockSpec(memory_space=pl.ANY)
    dma = pltpu.SemaphoreType.DMA
    return pl.pallas_call(
        functools.partial(moe_kernel, group),
        out_shape=jax.ShapeDtypeStruct((tokens, width), BF16),
        in_specs=[hbm] * 11,
        out_specs=vmem,
        scratch_shapes=[
            pltpu.VMEM(queries.shape, BF16),
            pltpu.VMEM(keys.shape, BF16),
            pltpu.VMEM(values.shape, BF16),
            pltpu.VMEM((wave, 1, group * tokens), jnp.int32),
            pltpu.VMEM(res.shape, BF16),
            pltpu.VMEM((1, width), F32),
            pltpu.VMEM(routes.shape[::-1], jnp.int32),
            pltpu.VMEM(gates.shape[::-1], F32),
            dma((8,)),
            pltpu.VMEM((wave, tokens, 2 * HEAD_DIM), BF16),
            pltpu.VMEM((wave, group, tokens, 2 * HEAD_DIM), BF16),
            pltpu.VMEM((wave, group * tokens, 128), F32),
            pltpu.VMEM((wave, group, tokens, queries.shape[1]), BF16),
            pltpu.VMEM((wave, group, tokens, queries.shape[1]), BF16),
            pltpu.VMEM((wave, group, tokens, queries.shape[1]), BF16),
            dma((wave,)), dma((wave, group)), dma((wave, group)),
            dma((wave,)), dma((wave,)), dma((wave, group)), dma((wave, group)),
            pltpu.VMEM((2 * wg.shape[0], width), BF16),
            pltpu.VMEM((wd.shape[0], width), BF16),
            pltpu.VMEM((wave, 2 * capacity, half), BF16),
            pltpu.VMEM((group, wave, 2 * capacity, half), BF16),
            pltpu.VMEM((group, wave, 2 * capacity, half), BF16),
            pltpu.VMEM((pairs, wave, 2 * capacity, half), BF16),
            pltpu.VMEM((pairs, wave, 2 * capacity, half), BF16),
            pltpu.VMEM((pairs, wave, 2 * capacity, half), BF16),
            pltpu.VMEM((wave, 2 * capacity, half), BF16),
            pltpu.VMEM((wave, 2 * capacity, half), BF16),
            dma((3,)), dma((wave,)), dma((group, wave)), dma((group, wave)),
            dma((pairs,)), dma((pairs,)), dma((pairs, wave)), dma((pairs, wave)), dma((wave,)), dma((wave,)),
        ],
        compiler_params=pltpu.CompilerParams(
            collective_id=0, has_side_effects=True, vmem_limit_bytes=60 * 2**20
        ),
    )(queries, keys, values, span_ids.reshape(wave, 1, group * tokens), res, gain.reshape(1, width), routes.T, gates.T, wg, wu, wd)


def solution(mesh):
    return jax.shard_map(
        layer,
        mesh=mesh,
        in_specs=(
            P("dp", "expert"),
            P(("dp", "expert"), None),
            P(("dp", "expert"), None),
            P("dp"),
            P(("dp", "expert"), None),
            P(),
            P(("dp", "expert"), None),
            P(("dp", "expert"), None),
            P("expert", None),
            P("expert", None),
            P("expert", None),
        ),
        out_specs=P(("dp", "expert"), None),
        check_vma=False,
    )
```

profile of v0, /device:TPU:0, one launch (start us, length us, event | category | flops | bytes accessed | tf_op | source)
XLA Modules:
  0.0 64.5 jit_solution(17689656069844813894)
XLA Ops:
  0.0 62.8 %shard_map.109 = bf16[32,4096]{1,0:T(8,128)(2,1)} custom-call(bf16[1024,128]{1,0:T(8,128)(2,1)} %queries_hbm.1, bf16[32,256]{1,0:T(8,128)(2,1)} %keys_hbm.1, bf16[32,256]{1,0:T(8,128)(2,1)} %values_hbm.1, s32[4,1,256]{2,1,0:T(1,128)} %bitcast.5, bf16[32,4096]{1,0:T(8,128)(2,1)} %res_hbm.1, f32[1,4096]{1,0:T(1,128)} %bitcast.4, s32[8,32]{1,0:T(8,128)} %bitcast.6, ...), custom_call_target="tpu_custom_call" | custom-call | tf_op jit(solution)/shard_map/pallas_call | solution.py:288
  62.8 1.7 %copy.13 = bf16[32,4096]{1,0:T(8,128)(2,1)} copy(bf16[32,4096]{1,0:T(8,128)(2,1)} %shard_map.109) | data formatting | bytes 524288
where the time goes:
time: 64.7 us; the launch traced here: 64.5 us
  Pallas kernels  62.8 us (97%)
  local copies, waits for them, and re-layouts  1.67 us (3%)
    pallas_call x1, Pallas kernels, layer(): pl.pallas_call(functools.partial(moe_kernel, group), out_shape=jax.ShapeD...  62.8 us
    unnamed x1, local copies, waits for them, and re-layouts  1.67 us

commit v1 on v0

v1 whole, which is shorter than its diff:
```python
import functools
import math

import jax
import jax.numpy as jnp
from jax import lax
from jax.experimental import pallas as pl
from jax.experimental.pallas import tpu as pltpu
from jax.sharding import PartitionSpec as P

KV_HEADS = 4
HEAD_DIM = 64
FF_WIN = 1024
SPAN = 512
CHUNKS = 4
MESH = pl.DeviceIdType.MESH
F32 = jnp.float32
BF16 = jnp.bfloat16


def remote(src, dst, send, recv, device):
    return pltpu.make_async_remote_copy(
        src_ref=src, dst_ref=dst, send_sem=send, recv_sem=recv,
        device_id={"expert": device}, device_id_type=MESH,
    )


def arrived(ref, sem):
    pltpu.make_async_copy(ref, ref, sem).wait()


def route_matrix(routes, gates, wave, capacity):
    tokens = routes.shape[0]
    here = tokens // 2
    columns = wave * 2 * capacity
    column = lax.broadcasted_iota(jnp.int32, (tokens, columns), 1)
    token = lax.broadcasted_iota(jnp.int32, (tokens, columns), 0)
    one = lax.broadcasted_iota(jnp.int32, (tokens, tokens), 0)
    other = lax.broadcasted_iota(jnp.int32, (tokens, tokens), 1)
    lower = jnp.where((one >= other) & (one // here == other // here), 1.0, 0.0)
    named_wide = jnp.zeros((tokens, columns), F32)
    weight_wide = jnp.zeros((tokens, columns), F32)
    for expert in range(wave):
        hits = routes == expert
        named = jnp.max(jnp.where(hits, 1.0, 0.0), axis=1, keepdims=True)
        weight = jnp.sum(jnp.where(hits, gates, 0.0), axis=1, keepdims=True)
        mask = column // (2 * capacity) == expert
        named_wide = jnp.where(mask, named, named_wide)
        weight_wide = jnp.where(mask, weight, weight_wide)
    count = jnp.dot(lower.astype(BF16), named_wide.astype(BF16), preferred_element_type=F32)
    slot = (column % capacity + 1).astype(F32)
    fits = (count == slot) & (column % (2 * capacity) // capacity == token // here)
    chosen = jnp.where(fits, named_wide, 0.0)
    return chosen, chosen * weight_wide


def moe_kernel(names, group, *refs):
    at = dict(zip(names, refs, strict=True))
    (queries, keys, values, ids, res, gain, routes, gates, wg, wu, wd, out) = (
        at[name] for name in ("queries", "keys", "values", "ids", "res", "gain", "routes", "gates", "wg", "wu", "wd", "out")
    )
    (keys_v, values_v, ids_v, gain_v, routes_v, gates_v, rg_v, res_v, w_v, wd_v) = (
        at[name] for name in ("keys_v", "values_v", "ids_v", "gain_v", "routes_v", "gates_v", "rg_v", "res_v", "w_v", "wd_v")
    )
    (kv_pack, kv_far, kv_buf, q_buf, bias_v, stream_v, outg, x_buf, pre_out, pre_in) = (
        at[name] for name in ("kv_pack", "kv_far", "kv_buf", "q_buf", "bias_v", "stream_v", "outg", "x_buf", "pre_out", "pre_in")
    )
    (s1, r1, s2, r2, keep, own, final, back, out_v) = (
        at[name] for name in ("s1", "r1", "s2", "r2", "keep", "own", "final", "back", "out_v")
    )
    (in_sem, w_sem, ready_sem, send_sem, kv_sem, q_sem, pair_sem, z_sem, x_sem, pre_sem, r1_sem, r2_sem, back_sem, out_sem) = (
        at[name] for name in (
            "in_sem", "w_sem", "ready_sem", "send_sem", "kv_sem", "q_sem", "pair_sem", "z_sem", "x_sem",
            "pre_sem", "r1_sem", "r2_sem", "back_sem", "out_sem")
    )
    me = lax.axis_index("expert")
    wave = x_buf.shape[2]
    devices = wave * group
    tokens, width = out.shape
    both = 2 * tokens
    half = width // 2
    quarter = half // 2
    block = half // CHUNKS
    rows = wave * 16
    plane = me // group
    mine = me % group
    core = me % 2
    other = 1 - core
    here = pl.ds(pl.multiple_of(core * half, 128), half)
    there = pl.ds(pl.multiple_of(other * half, 128), half)

    def across(rz):
        return (plane ^ rz) * group + mine

    def within(r):
        return plane * group + (mine ^ r)

    partner = within(1)
    fetched = {}
    for number, (name, source, target) in enumerate((
        ("keys", keys, keys_v), ("values", values, values_v), ("routes", routes, routes_v), ("gates", gates, gates_v),
        ("ids", ids, ids_v), ("gain", gain.at[:, here], gain_v),
    )):
        fetched[name] = pltpu.make_async_copy(source, target, in_sem.at[number])
        fetched[name].start()
    barrier = pltpu.get_barrier_semaphore()
    partners = [within(r) for r in range(1, group)] + [across(rz) for rz in range(1, wave)]
    for device in partners:
        pl.semaphore_signal(barrier, inc=1, device_id={"expert": device}, device_id_type=MESH)
    pltpu.make_async_copy(res.at[:, here], res_v.at[core], pair_sem.at[1]).start()
    pltpu.make_async_copy(wg.at[:, here], w_v.at[0, core], w_sem.at[0]).start()
    pltpu.make_async_copy(wu.at[:, here], w_v.at[1, core], w_sem.at[0]).start()
    pltpu.make_async_copy(wd.at[:, here], wd_v.at[core], w_sem.at[1]).start()
    for name in ("keys", "values", "routes", "gates"):
        fetched[name].wait()
    for head in range(KV_HEADS):
        columns = slice(head * HEAD_DIM, (head + 1) * HEAD_DIM)
        kv_pack[head] = jnp.concatenate([keys_v[:, columns], values_v[:, columns]], axis=1)
    rg_v[core, :8, :tokens] = routes_v[...].astype(F32)
    rg_v[core, 8:, :tokens] = gates_v[...]
    pl.semaphore_wait(barrier, len(partners))

    sends = []

    def go(src, dst, recv, device):
        copy = remote(src, dst, send_sem, recv, device)
        copy.start()
        sends.append(copy)

    planes = SPAN // (group * tokens)
    halves = KV_HEADS // 2
    for rz in range(1, planes):
        go(kv_pack, kv_far.at[rz - 1], kv_sem.at[0], across(rz))
    for rz in range(1, wave):
        pl.semaphore_signal(ready_sem, inc=1, device_id={"expert": across(rz)}, device_id_type=MESH)
    for r in range(1, group):
        which = (core ^ (r % 2)) * halves
        go(kv_pack.at[pl.ds(which, halves)], kv_buf.at[plane % planes, mine], kv_sem.at[1], within(r))
    kv_buf[plane % planes, mine] = kv_pack[pl.ds(core * halves, halves)]
    go(rg_v.at[core], rg_v.at[core], pair_sem.at[0], partner)
    pl.semaphore_wait(ready_sem, wave - 1)
    side = me // (devices // 2)
    number = me % (devices // 2)
    per_chunk = devices // 2 // CHUNKS
    query_sem = q_sem.at[number // per_chunk]
    for r in range(devices // 2 - 1, 0, -1):
        pair = (me // 2) ^ r
        source = queries.at[pl.ds(pl.multiple_of(pair * both, both), both)]
        go(source, q_buf.at[number], query_sem, pair * 2 + side)
    source = queries.at[pl.ds(pl.multiple_of(me // 2 * both, both), both)]

    @pl.when(core == side)
    def _():
        pltpu.make_async_copy(source, q_buf.at[number], query_sem).start()

    @pl.when(core != side)
    def _():
        remote(source, q_buf.at[number], at["self_sem"], query_sem, partner).start()

    for rz in range(1, planes):
        arrived(kv_far.at[rz - 1], kv_sem.at[0])
        for r in range(1, group):
            which = (core ^ (r % 2)) * halves
            go(kv_far.at[rz - 1, pl.ds(which, halves)], kv_buf.at[(plane ^ rz) % planes, mine], kv_sem.at[2], within(r))
        kv_buf[(plane ^ rz) % planes, mine] = kv_far[rz - 1, pl.ds(core * halves, halves)]
    go(res.at[:, there], res_v.at[core], pair_sem.at[1], partner)
    go(wg.at[:, there], w_v.at[0, core], w_sem.at[0], partner)
    go(wu.at[:, there], w_v.at[1, core], w_sem.at[0], partner)
    go(wd.at[:, there], wd_v.at[core], w_sem.at[1], partner)
    fetched["ids"].wait()
    arrived(rg_v.at[0], pair_sem.at[0])
    named = jnp.concatenate([rg_v[c, :8, :].T[:tokens] for c in range(2)], axis=0)
    weights = jnp.concatenate([rg_v[c, 8:, :].T[:tokens] for c in range(2)], axis=0)
    chosen, mix = route_matrix(named, weights, wave, 8)
    chosen = chosen.T.astype(BF16)

    stretch = group * tokens
    wide = per_chunk * both
    first = plane // planes * planes
    key_ids = jnp.concatenate(
        [jnp.broadcast_to(ids_v[first + i].astype(F32), (128, stretch)).T for i in range(planes)], axis=0
    )
    key_ids = jnp.concatenate([key_ids] * (wide // 128), axis=1)
    key_at = lax.broadcasted_iota(jnp.int32, (SPAN, wide), 0)
    query_at = (
        lax.broadcasted_iota(jnp.int32, (SPAN, wide), 1) % both
        + ((plane - first) * stretch + mine // 2 * both)
    )
    query_ids = jnp.sum(jnp.where(key_at == query_at, key_ids, 0.0), axis=0, keepdims=True)
    bias_v[...] = jnp.where((key_at <= query_at) & (key_ids == query_ids), 0.0, -jnp.inf)
    arrived(kv_buf.at[0, pl.ds(0, group - 1)], kv_sem.at[1])
    if planes > 1:
        arrived(kv_buf.at[pl.ds(0, planes - 1), pl.ds(0, group - 1)], kv_sem.at[2])

    def attend(g):
        head = g * halves // CHUNKS
        held = kv_buf[:, :, head].reshape(SPAN, 2 * HEAD_DIM)
        key_blk = held[:, :HEAD_DIM]
        value_rows = held.T[HEAD_DIM:]
        query = q_buf[g * per_chunk:(g + 1) * per_chunk].reshape(wide, -1) * BF16(1.0 / math.sqrt(HEAD_DIM))
        heads = []
        for number in range(query.shape[1] // HEAD_DIM):
            one = query[:, number * HEAD_DIM:(number + 1) * HEAD_DIM]
            scores = lax.dot_general(key_blk, one, (((1,), (1,)), ((), ())), preferred_element_type=F32)
            scores = scores + bias_v[...]
            raised = jnp.exp(scores - jnp.max(scores, axis=0, keepdims=True))
            total = jnp.sum(raised, axis=0, keepdims=True)
            heads.append(jnp.dot(value_rows, raised.astype(BF16), preferred_element_type=F32) * (1.0 / total))
        joined = heads[0] if len(heads) == 1 else jnp.concatenate(heads, axis=0)
        joined = joined.T.astype(BF16)
        return jnp.concatenate([joined[i * both:(i + 1) * both] for i in range(per_chunk)], axis=1)

    low, high = pl.ds(0, wave // 2), pl.ds(wave // 2, wave - wave // 2)
    parts = (low, high)
    near = (within(2), within(4))

    def forward(g):
        for part in range(2):
            if part:
                arrived(x_buf.at[g, 0, high], z_sem.at[g, 1])
            elif wave > 2:
                arrived(x_buf.at[g, 0, pl.ds(1, wave // 2 - 1)], z_sem.at[g, 0])
            piece = x_buf.at[g, 0, parts[part]]
            for hop in range(2):
                go(piece, x_buf.at[g, 1 + hop, parts[part]], x_sem.at[g, hop, part], near[hop])

    def relay(g):
        for hop in range(2):
            piece = x_buf.at[g, 1 + hop, parts[hop]]
            arrived(piece, x_sem.at[g, hop, hop])
            go(piece, x_buf.at[g, 3, parts[hop]], x_sem.at[g, 2, hop], near[1 - hop])

    for g in range(CHUNKS):
        arrived(q_buf.at[pl.ds(g * per_chunk, per_chunk)], q_sem.at[g])
        if g == 0:
            arrived(res_v, pair_sem.at[1])
        columns = slice(g * block, (g + 1) * block)
        attended = attend(g)
        stream = (res_v[:, :, columns].reshape(both, block).astype(F32) + attended.astype(F32)).astype(BF16)
        stream_v[g] = stream
        outg[g] = jnp.dot(chosen, stream, preferred_element_type=F32).astype(BF16).reshape(wave, 16, block)
        for rz in range(wave - 1, 0, -1):
            go(outg.at[g, plane ^ rz], x_buf.at[g, 0, rz], z_sem.at[g, rz // (wave // 2)], across(rz))
        x_buf[g, 0, 0] = outg[g, plane]
        if g >= 2:
            forward(g - 2)
    fetched["gain"].wait()
    arrived(w_v, w_sem.at[0])

    squares = None
    pre = None

    def up(g):
        for hop in range(2):
            arrived(x_buf.at[g, 1 + hop, parts[1 - hop]], x_sem.at[g, hop, 1 - hop])
            arrived(x_buf.at[g, 3, parts[hop]], x_sem.at[g, 2, hop])
        columns = slice(g * block, (g + 1) * block)
        x = x_buf[g].reshape(4 * rows, block).astype(F32)
        square = x * x
        square = sum(square[:, i:i + 128] for i in range(0, block, 128))
        x = (x * gain_v[:, columns]).astype(BF16)
        weight = w_v[:, :, :, columns].reshape(-1, block)
        return square, lax.dot_general(x, weight, (((1,), (1,)), ((), ())), preferred_element_type=F32)

    steps = [(forward, CHUNKS - 2), (relay, 0), (forward, CHUNKS - 1)]
    for g in range(CHUNKS):
        if g + 1 < CHUNKS:
            steps.append((relay, g + 1))
        steps.append((up, g))
    for step, g in steps:
        result = step(g)
        if result is not None:
            squares = result[0] if squares is None else squares + result[0]
            pre = result[1] if pre is None else pre + result[1]
    units = pre.shape[1]
    square = jnp.sum(squares, axis=1, keepdims=True)
    coarse = square.astype(BF16)
    rest = (square - coarse.astype(F32)).astype(BF16)
    lane = lax.broadcasted_iota(jnp.int32, (4 * rows, 128), 1)
    pre_out[:, :units] = pre.astype(BF16)
    pre_out[:, units:] = jnp.where(lane < 64, coarse.astype(F32), rest.astype(F32)).astype(BF16)
    go(pre_out, pre_in, pre_sem, partner)
    arrived(pre_in, pre_sem)
    square = square + pre_in[:, units:units + 1].astype(F32) + pre_in[:, units + 64:units + 65].astype(F32)
    inverse = lax.rsqrt(square * (1.0 / width) + 1e-06)
    pre = (pre + pre_in[:, :units].astype(F32)) * inverse
    gate_pre, up_pre = pre[:, :units // 2], pre[:, units // 2:]
    hidden = (gate_pre / (1.0 + jnp.exp(-gate_pre)) * up_pre).astype(BF16)
    arrived(wd_v, w_sem.at[1])

    def down(blk):
        weight = wd_v[...].reshape(-1, half)
        piece = jnp.dot(hidden[blk * rows:(blk + 1) * rows], weight, preferred_element_type=F32)
        return piece.reshape(wave, 16, half)

    def first_hop(which, kind, piece):
        s1[which, kind] = piece.astype(BF16)
        for part in (1, 0):
            go(s1.at[which, kind, parts[part]], r1.at[which, kind, parts[part]], r1_sem.at[which, kind, part], near[which])

    piece = down(3)
    first_hop(0, 0, piece[:, :, :quarter])
    first_hop(1, 0, piece[:, :, quarter:])
    piece = down(1)
    first_hop(0, 1, piece[:, :, :quarter])
    keep[1] = piece[:, :, quarter:]
    piece = down(2)
    first_hop(1, 1, piece[:, :, quarter:])
    keep[0] = piece[:, :, :quarter]
    piece = down(0)
    own[0] = piece[:, :, :quarter]
    own[1] = piece[:, :, quarter:]
    for part in (1, 0):
        for which in range(2):
            chunk = parts[part]
            arrived(r1.at[which, 0, chunk], r1_sem.at[which, 0, part])
            s2[which, chunk] = (keep[which, chunk] + r1[which, 0, chunk].astype(F32)).astype(BF16)
            go(s2.at[which, chunk], r2.at[which, chunk], r2_sem.at[which, part], near[1 - which])
    for part in (1, 0):
        chunk = parts[part]
        for which in range(2):
            arrived(r1.at[which, 1, chunk], r1_sem.at[which, 1, part])
            arrived(r2.at[which, chunk], r2_sem.at[which, part])
            total = own[which, chunk] + r1[which, 1, chunk].astype(F32) + r2[which, chunk].astype(F32)
            final[chunk, :, which * quarter:(which + 1) * quarter] = total.astype(BF16)
        for rz in range((part + 1) * (wave // 2) - 1, part * (wave // 2) - 1, -1):
            if rz:
                go(final.at[rz], back.at[plane], back_sem, across(rz))
            else:
                back[plane] = final[0]
    arrived(back.at[pl.ds(0, wave - 1)], back_sem)
    high_mix = mix.astype(BF16)
    rest = mix - high_mix.astype(F32)
    middle = rest.astype(BF16)
    lowest = (rest - middle.astype(F32)).astype(BF16)
    for g in range(CHUNKS):
        columns = slice(g * block, (g + 1) * block)
        outs = back[:, :, columns].reshape(rows, block)
        added = (
            jnp.dot(lowest, outs, preferred_element_type=F32)
            + jnp.dot(middle, outs, preferred_element_type=F32)
            + jnp.dot(high_mix, outs, preferred_element_type=F32)
        )
        out_v[:, :, columns] = (stream_v[g].astype(F32) + added).astype(BF16).reshape(2, tokens, block)
    go(out_v.at[other], out.at[:, here], out_sem.at[0], partner)
    copy = pltpu.make_async_copy(out_v.at[core], out.at[:, here], out_sem.at[1])
    copy.start()
    copy.wait()
    arrived(out.at[:, there], out_sem.at[0])

    @pl.when(core != side)
    def _():
        remote(source, q_buf.at[number], at["self_sem"], query_sem, partner).wait_send()

    for copy in sends:
        copy.wait_send()


def layer(queries, keys, values, span_ids, res, gain, routes, gates, wg, wu, wd):
    devices = lax.axis_size("expert")
    group = FF_WIN // wg.shape[0]
    wave = devices // group
    tokens, width = res.shape
    half = width // 2
    hidden = wg.shape[0]
    both = 2 * tokens
    block = half // CHUNKS
    planes = SPAN // (group * tokens)
    halves = KV_HEADS // 2
    rows = wave * 16
    per_chunk = devices // 2 // CHUNKS
    hbm = pl.BlockSpec(memory_space=pl.ANY)
    dma = pltpu.SemaphoreType.DMA

    def vmem(*shape, dtype=BF16):
        return pltpu.VMEM(shape, dtype)

    scratch = {
        "keys_v": vmem(*keys.shape),
        "values_v": vmem(*values.shape),
        "ids_v": vmem(wave, 1, group * tokens, dtype=jnp.int32),
        "gain_v": vmem(1, half, dtype=F32),
        "routes_v": vmem(*routes.shape[::-1], dtype=jnp.int32),
        "gates_v": vmem(*gates.shape[::-1], dtype=F32),
        "rg_v": vmem(2, 16, 128, dtype=F32),
        "res_v": vmem(2, tokens, half),
        "w_v": vmem(2, 2, hidden, half),
        "wd_v": vmem(2, hidden, half),
        "kv_pack": vmem(KV_HEADS, tokens, 2 * HEAD_DIM),
        "kv_far": vmem(max(planes - 1, 1), KV_HEADS, tokens, 2 * HEAD_DIM),
        "kv_buf": vmem(planes, group, halves, tokens, 2 * HEAD_DIM),
        "q_buf": vmem(devices // 2, both, queries.shape[1]),
        "bias_v": vmem(SPAN, per_chunk * both, dtype=F32),
        "stream_v": vmem(CHUNKS, both, block),
        "outg": vmem(CHUNKS, wave, 16, block),
        "x_buf": vmem(CHUNKS, 4, wave, 16, block),
        "pre_out": vmem(4 * rows, 4 * hidden + 128),
        "pre_in": vmem(4 * rows, 4 * hidden + 128),
        "s1": vmem(2, 2, wave, 16, half // 2),
        "r1": vmem(2, 2, wave, 16, half // 2),
        "s2": vmem(2, wave, 16, half // 2),
        "r2": vmem(2, wave, 16, half // 2),
        "keep": vmem(2, wave, 16, half // 2, dtype=F32),
        "own": vmem(2, wave, 16, half // 2, dtype=F32),
        "final": vmem(wave, 16, half),
        "back": vmem(wave, 16, half),
        "out_v": vmem(2, tokens, half),
        "in_sem": dma((6,)),
        "w_sem": dma((2,)),
        "ready_sem": pltpu.SemaphoreType.REGULAR,
        "send_sem": dma(()),
        "self_sem": dma(()),
        "kv_sem": dma((3,)),
        "q_sem": dma((CHUNKS,)),
        "pair_sem": dma((2,)),
        "z_sem": dma((CHUNKS, 2)),
        "x_sem": dma((CHUNKS, 3, 2)),
        "pre_sem": dma(()),
        "r1_sem": dma((2, 2, 2)),
        "r2_sem": dma((2, 2)),
        "back_sem": dma(()),
        "out_sem": dma((2,)),
    }
    names = ("queries", "keys", "values", "ids", "res", "gain", "routes", "gates", "wg", "wu", "wd", "out", *scratch)
    return pl.pallas_call(
        functools.partial(moe_kernel, names, group),
        out_shape=jax.ShapeDtypeStruct((tokens, width), BF16),
        in_specs=[hbm] * 11,
        out_specs=hbm,
        scratch_shapes=list(scratch.values()),
        compiler_params=pltpu.CompilerParams(
            collective_id=0, has_side_effects=True, vmem_limit_bytes=60 * 2**20
        ),
    )(
        queries, keys, values, span_ids.reshape(wave, 1, group * tokens), res, gain.reshape(1, width),
        routes.T, gates.T, wg, wu, wd,
    )


def solution(mesh):
    return jax.shard_map(
        layer,
        mesh=mesh,
        in_specs=(
            P("dp", "expert"),
            P(("dp", "expert"), None),
            P(("dp", "expert"), None),
            P("dp"),
            P(("dp", "expert"), None),
            P(),
            P(("dp", "expert"), None),
            P(("dp", "expert"), None),
            P("expert", None),
            P("expert", None),
            P("expert", None),
        ),
        out_specs=P(("dp", "expert"), None),
        check_vma=False,
    )
```

time: 64.7 us -> 52.9 us (0.82)
  Pallas kernels: 62.8 us -> 50.9 us
    pallas_call x1, Pallas kernels: 62.8 us -> 50.9 us  [layer(): pl.pallas_call(functools.partial(moe_kernel, names, group), out_shape=jax...]
where the time goes in v1:
time: 52.9 us; the launch traced here: 52.6 us
  Pallas kernels  50.9 us (96%)
  local copies, waits for them, and re-layouts  1.67 us (3%)
    pallas_call x1, Pallas kernels, layer(): pl.pallas_call(functools.partial(moe_kernel, names, group), out_shape=jax...  50.9 us
    unnamed x1, local copies, waits for them, and re-layouts  1.67 us

profile of v1, /device:TPU:0, one launch (start us, length us, event | category | flops | bytes accessed | tf_op | source)
XLA Modules:
  0.0 52.6 jit_solution(3080095049991343809)
XLA Ops:
  0.0 50.9 %shard_map.109 = bf16[32,4096]{1,0:T(8,128)(2,1)} custom-call(bf16[1024,128]{1,0:T(8,128)(2,1)} %refs_0_.1, bf16[32,256]{1,0:T(8,128)(2,1)} %refs_1_.1, bf16[32,256]{1,0:T(8,128)(2,1)} %refs_2_.1, s32[4,1,256]{2,1,0:T(1,128)} %bitcast.5, bf16[32,4096]{1,0:T(8,128)(2,1)} %refs_4_.1, f32[1,4096]{1,0:T(1,128)} %bitcast.4, s32[8,32]{1,0:T(8,128)} %bitcast.6, ...), custom_call_target="tpu_custom_call" | custom-call | tf_op jit(solution)/shard_map/pallas_call | solution.py:425
  51.0 1.7 %copy.13 = bf16[32,4096]{1,0:T(8,128)(2,1)} copy(bf16[32,4096]{1,0:T(8,128)(2,1)} %shard_map.109) | data formatting | bytes 524288

commit v2 on v1

v2 whole, which is shorter than its diff:
```python
import functools
import math

import jax
import jax.numpy as jnp
from jax import lax
from jax.experimental import pallas as pl
from jax.experimental.pallas import tpu as pltpu
from jax.sharding import PartitionSpec as P

KV_HEADS = 4
HEAD_DIM = 64
FF_WIN = 1024
SPAN = 512
CHUNKS = 4
WINDOW = 3
MESH = pl.DeviceIdType.MESH
F32 = jnp.float32
BF16 = jnp.bfloat16


def remote(src, dst, send, recv, device):
    return pltpu.make_async_remote_copy(
        src_ref=src, dst_ref=dst, send_sem=send, recv_sem=recv,
        device_id={"expert": device}, device_id_type=MESH,
    )


def arrived(ref, sem):
    pltpu.make_async_copy(ref, ref, sem).wait()


def route_matrix(routes, gates, wave, capacity, cores):
    tokens = routes.shape[0]
    here = tokens // cores
    columns = wave * cores * capacity
    column = lax.broadcasted_iota(jnp.int32, (tokens, columns), 1)
    token = lax.broadcasted_iota(jnp.int32, (tokens, columns), 0)
    one = lax.broadcasted_iota(jnp.int32, (tokens, tokens), 0)
    other = lax.broadcasted_iota(jnp.int32, (tokens, tokens), 1)
    lower = jnp.where((one >= other) & (one // here == other // here), 1.0, 0.0)
    named_wide = jnp.zeros((tokens, columns), F32)
    weight_wide = jnp.zeros((tokens, columns), F32)
    for expert in range(wave):
        hits = routes == expert
        named = jnp.max(jnp.where(hits, 1.0, 0.0), axis=1, keepdims=True)
        weight = jnp.sum(jnp.where(hits, gates, 0.0), axis=1, keepdims=True)
        mask = column // (cores * capacity) == expert
        named_wide = jnp.where(mask, named, named_wide)
        weight_wide = jnp.where(mask, weight, weight_wide)
    count = jnp.dot(lower.astype(BF16), named_wide.astype(BF16), preferred_element_type=F32)
    slot = (column % capacity + 1).astype(F32)
    fits = (count == slot) & (column % (cores * capacity) // capacity == token // here)
    chosen = jnp.where(fits, named_wide, 0.0)
    return chosen, chosen * weight_wide


def moe_kernel(names, group, *refs):
    at = dict(zip(names, refs, strict=True))
    (queries, keys, values, ids, res, gain, routes, gates, wg, wu, wd, out) = (
        at[name] for name in ("queries", "keys", "values", "ids", "res", "gain", "routes", "gates", "wg", "wu", "wd", "out")
    )
    (keys_v, values_v, ids_v, gain_v, routes_v, gates_v, rg_v, res_v, w_v, wd_v) = (
        at[name] for name in ("keys_v", "values_v", "ids_v", "gain_v", "routes_v", "gates_v", "rg_v", "res_v", "w_v", "wd_v")
    )
    (kv_pack, kv_far, kv_buf, q_buf, bias_v, stream_v, stream_all, outg, x_buf, pre_out, pre_in) = (
        at[name] for name in (
            "kv_pack", "kv_far", "kv_buf", "q_buf", "bias_v", "stream_v", "stream_all", "outg", "x_buf", "pre_out", "pre_in")
    )
    (s1, r1, s2, r2, keep, own, final, back) = (
        at[name] for name in ("s1", "r1", "s2", "r2", "keep", "own", "final", "back")
    )
    (far_sem, in_sem, w_sem, ready_sem, send_sem, kv_sem, q_sem, pair_sem, z_sem, x_sem, pre_sem, r1_sem, r2_sem, back_sem) = (
        at[name] for name in (
            "far_sem", "in_sem", "w_sem", "ready_sem", "send_sem", "kv_sem", "q_sem", "pair_sem", "z_sem", "x_sem",
            "pre_sem", "r1_sem", "r2_sem", "back_sem")
    )
    me = lax.axis_index("expert")
    wave = x_buf.shape[2]
    devices = wave * group
    tokens, width = out.shape
    both = 2 * tokens
    half = width // 2
    quarter = half // 2
    block = half // CHUNKS
    rows = wave * 16
    plane = me // group
    mine = me % group
    core = me % 2
    other = 1 - core


    sends = []

    def go(src, dst, recv, device):
        copy = remote(src, dst, send_sem, recv, device)
        copy.start()
        sends.append(copy)

    def early(c):
        return [pl.ds(pl.multiple_of(q * quarter, 128), quarter) for q in (1 + c, 3 * c)]

    def split(source, target, sem, send):
        for n, columns in enumerate(early(core if send is None else other)):
            place = target.at[:, pl.ds(n * quarter, quarter)]
            if send is None:
                pltpu.make_async_copy(source.at[:, columns], place, sem).start()
            else:
                go(source.at[:, columns], place, sem, send)

    def across(rz):
        return (plane ^ rz) * group + mine

    def within(r):
        return plane * group + (mine ^ r)

    partner = within(1)
    fetched = {}
    for number, (name, source, target) in enumerate((
        ("keys", keys, keys_v), ("values", values, values_v), ("routes", routes, routes_v), ("gates", gates, gates_v),
        ("ids", ids, ids_v),
    )):
        fetched[name] = pltpu.make_async_copy(source, target, in_sem.at[number])
        fetched[name].start()
    barrier = pltpu.get_barrier_semaphore()
    partners = [within(r) for r in range(1, group)] + [across(rz) for rz in range(1, wave)]
    for device in partners:
        pl.semaphore_signal(barrier, inc=1, device_id={"expert": device}, device_id_type=MESH)
    split(res, res_v.at[core], pair_sem.at[1], None)
    split(gain, gain_v, in_sem.at[5], None)
    split(wg, w_v.at[0, core], w_sem.at[0], None)
    split(wu, w_v.at[1, core], w_sem.at[0], None)
    split(wd, wd_v.at[core], w_sem.at[1], None)
    pl.semaphore_wait(barrier, len(partners))
    for rz in range(1, wave):
        pl.semaphore_signal(ready_sem, inc=1, device_id={"expert": across(rz)}, device_id_type=MESH)

    for name in ("keys", "values"):
        fetched[name].wait()
    for place, head in enumerate((1, 2, 0, 3)):
        columns = slice(head * HEAD_DIM, (head + 1) * HEAD_DIM)
        kv_pack[place] = jnp.concatenate([keys_v[:, columns], values_v[:, columns]], axis=1)
    planes = SPAN // (group * tokens)
    halves = KV_HEADS // 2
    for h in range(halves):
        for rz in range(1, planes):
            pair = pl.ds(2 * h, 2)
            go(kv_pack.at[pair], kv_far.at[rz - 1, pair], far_sem.at[rz - 1, h], across(rz))

    def share(h, source, at_plane, sem):
        for r in range(1, group):
            go(source.at[2 * h + (core ^ (r % 2))], kv_buf.at[h, at_plane, mine], sem, within(r))
        kv_buf[h, at_plane, mine] = source[2 * h + core]

    share(0, kv_pack, plane % planes, kv_sem.at[0, 0])
    pl.semaphore_wait(ready_sem, wave - 1)
    side = me // (devices // 2)
    number = (me % (devices // 2)) ^ ((1 - side) * (devices // 4))
    per_chunk = devices // 2 // CHUNKS
    query_sem = q_sem.at[number // per_chunk]

    def ask(r):
        pair = (me // 2) ^ r
        source = queries.at[pl.ds(pl.multiple_of(pair * both, both), both)]
        return remote(source, q_buf.at[number], at["ask_sem"], query_sem, pair * 2 + side)

    def ask_all():
        for r in range(devices // 2 - 1, 0, -1):
            ask(r).start()

        @pl.when(core == side)
        def _():
            source = queries.at[pl.ds(pl.multiple_of(me // 2 * both, both), both)]
            pltpu.make_async_copy(source, q_buf.at[number], query_sem).start()

        @pl.when(core != side)
        def _():
            ask(0).start()

    @pl.when(number < devices // 4)
    def _():
        ask_all()

    for name in ("routes", "gates"):
        fetched[name].wait()
    rg_v[core, :8, :tokens] = routes_v[...].astype(F32)
    rg_v[core, 8:, :tokens] = gates_v[...]
    go(rg_v.at[core], rg_v.at[core], pair_sem.at[0], partner)
    def pass_on(h):
        for rz in range(1, planes):
            arrived(kv_far.at[rz - 1, pl.ds(2 * h, 2)], far_sem.at[rz - 1, h])
            share(h, kv_far.at[rz - 1], (plane ^ rz) % planes, kv_sem.at[1, h])

    pass_on(0)
    split(res, res_v.at[core], pair_sem.at[1], partner)
    fetched["ids"].wait()
    _, mix = route_matrix(routes_v[...].astype(F32).T, gates_v[...].T, wave, 8, 1)
    arrived(rg_v.at[0], pair_sem.at[0])
    named = jnp.concatenate([rg_v[c, :8, :].T[:tokens] for c in range(2)], axis=0)
    weights = jnp.concatenate([rg_v[c, 8:, :].T[:tokens] for c in range(2)], axis=0)
    chosen, _ = route_matrix(named, weights, wave, 8, 2)
    chosen = chosen.T.astype(BF16)

    stretch = group * tokens
    wide = per_chunk * both
    first = plane // planes * planes
    key_ids = jnp.concatenate(
        [jnp.broadcast_to(ids_v[first + i].astype(F32), (128, stretch)).T for i in range(planes)], axis=0
    )
    key_ids = jnp.concatenate([key_ids] * (wide // 128), axis=1)
    key_at = lax.broadcasted_iota(jnp.int32, (SPAN, wide), 0)
    query_at = (
        lax.broadcasted_iota(jnp.int32, (SPAN, wide), 1) % both
        + ((plane - first) * stretch + mine // 2 * both)
    )
    query_ids = jnp.sum(jnp.where(key_at == query_at, key_ids, 0.0), axis=0, keepdims=True)
    bias_v[...] = jnp.where((key_at <= query_at) & (key_ids == query_ids), 0.0, -jnp.inf)
    share(1, kv_pack, plane % planes, kv_sem.at[0, 1])
    pass_on(1)

    @pl.when(number >= devices // 4)
    def _():
        ask_all()

    def gathered(h):
        arrived(kv_buf.at[h, 0, pl.ds(0, group - 1)], kv_sem.at[0, h])
        if planes > 1:
            arrived(kv_buf.at[h, pl.ds(0, planes - 1), pl.ds(0, group - 1)], kv_sem.at[1, h])

    gathered(0)
    split(wg, w_v.at[0, core], w_sem.at[0], partner)
    split(wu, w_v.at[1, core], w_sem.at[0], partner)
    split(wd, wd_v.at[core], w_sem.at[1], partner)

    def attend(g):
        head = g * halves // CHUNKS
        held = kv_buf[head].reshape(SPAN, 2 * HEAD_DIM)
        key_blk = held[:, :HEAD_DIM]
        value_rows = held.T[HEAD_DIM:]
        query = q_buf[g * per_chunk:(g + 1) * per_chunk].reshape(wide, -1) * BF16(1.0 / math.sqrt(HEAD_DIM))
        heads = []
        for number in range(query.shape[1] // HEAD_DIM):
            one = query[:, number * HEAD_DIM:(number + 1) * HEAD_DIM]
            scores = lax.dot_general(key_blk, one, (((1,), (1,)), ((), ())), preferred_element_type=F32)
            scores = scores + bias_v[...]
            raised = jnp.exp(scores - jnp.max(scores, axis=0, keepdims=True))
            total = jnp.sum(raised, axis=0, keepdims=True)
            heads.append(jnp.dot(value_rows, raised.astype(BF16), preferred_element_type=F32) * (1.0 / total))
        joined = heads[0] if len(heads) == 1 else jnp.concatenate(heads, axis=0)
        joined = joined.T.astype(BF16)
        return jnp.concatenate([joined[i * both:(i + 1) * both] for i in range(per_chunk)], axis=1)

    near = (within(2), within(4))

    def attention(g):
        if g == CHUNKS // halves:
            gathered(1)
        arrived(q_buf.at[pl.ds(g * per_chunk, per_chunk)], q_sem.at[g])
        if g == 0:
            arrived(res_v, pair_sem.at[1])
        columns = slice(g * block, (g + 1) * block)
        attended = attend(g)
        stream = (res_v[:, :, columns].reshape(both, block).astype(F32) + attended.astype(F32)).astype(BF16)
        stream_v[g] = stream
        outg[g] = jnp.dot(chosen, stream, preferred_element_type=F32).astype(BF16).reshape(wave, 16, block)

    def leave(g, rz):
        go(outg.at[g, plane ^ rz], x_buf.at[g, 0, rz], z_sem.at[g, rz], across(rz))

    def spread(g, rz):
        for hop in range(2):
            recv = x_sem.at[g, rz] if rz % 2 == hop else x_sem.at[g, wave]
            go(x_buf.at[g, 0, rz], x_buf.at[g, 1 + hop, rz], recv, near[hop])

    def forward(g, rz):
        arrived(x_buf.at[g, 0, rz], z_sem.at[g, rz])
        spread(g, rz)

    def relay(g, rz):
        hop = rz % 2
        piece = x_buf.at[g, 1 + hop, rz]
        arrived(piece, x_sem.at[g, rz])
        go(piece, x_buf.at[g, 3, rz], x_sem.at[g, wave], near[1 - hop])

    def tell(g):
        ours = pl.ds(pl.multiple_of(other * tokens, tokens), tokens)
        go(stream_v.at[g, ours], stream_all.at[core, g], pair_sem.at[2], partner)
        stream_all[core, g] = stream_v[g, pl.ds(pl.multiple_of(core * tokens, tokens), tokens)]
        x_buf[g, 0, 0] = outg[g, plane]
        spread(g, 0)

    total = {}

    def up(g):
        if g == 0:
            arrived(gain_v, in_sem.at[5])
            arrived(w_v, w_sem.at[0])
        arrived(x_buf.at[g, pl.ds(0, 2)], x_sem.at[g, wave])
        columns = slice(g * block, (g + 1) * block)
        x = x_buf[g].reshape(4 * rows, block).astype(F32)
        square = x * x
        square = sum(square[:, i:i + 128] for i in range(0, block, 128))
        x = (x * gain_v[:, columns]).astype(BF16)
        weight = w_v[:, :, :, columns].reshape(-1, block)
        pre = lax.dot_general(x, weight, (((1,), (1,)), ((), ())), preferred_element_type=F32)
        total["square"] = square if g == 0 else total["square"] + square
        total["pre"] = pre if g == 0 else total["pre"] + pre

    def offer():
        pre = total["pre"]
        units = pre.shape[1]
        square = jnp.sum(total["square"], axis=1, keepdims=True)
        total["square"] = square
        coarse = square.astype(BF16)
        rest = (square - coarse.astype(F32)).astype(BF16)
        lane = lax.broadcasted_iota(jnp.int32, (4 * rows, 128), 1)
        pre_out[:, :units] = pre.astype(BF16)
        pre_out[:, units:] = jnp.where(lane < 64, coarse.astype(F32), rest.astype(F32)).astype(BF16)
        go(pre_out, pre_in, pre_sem, partner)

    def hide():
        units = total["pre"].shape[1]
        arrived(pre_in, pre_sem)
        square = (
            total["square"] + pre_in[:, units:units + 1].astype(F32) + pre_in[:, units + 64:units + 65].astype(F32)
        )
        inverse = lax.rsqrt(square * (1.0 / width) + 1e-06)
        pre = (total["pre"] + pre_in[:, :units].astype(F32)) * inverse
        gate_pre, up_pre = pre[:, :units // 2], pre[:, units // 2:]
        total["hidden"] = (gate_pre / (1.0 + jnp.exp(-gate_pre)) * up_pre).astype(BF16)
        arrived(wd_v, w_sem.at[1])

    def product(blk):
        weight = wd_v[...].reshape(-1, half)
        piece = jnp.dot(total["hidden"][blk * rows:(blk + 1) * rows], weight, preferred_element_type=F32)
        piece = piece.reshape(wave, 16, half)
        return piece[:, :, :quarter], piece[:, :, quarter:]

    def first_hop(rz, sides=(0, 1)):
        for which in sides:
            go(s1.at[which, rz], r1.at[which, rz], r1_sem.at[which, rz], near[which])

    def down(early):
        one, two = product(3)
        s1[0, :, 0], s1[1, :, 0] = one.astype(BF16), two.astype(BF16)
        one, keep[1] = product(1)
        s1[0, :, 1] = one.astype(BF16)
        for rz in early:
            first_hop(rz, (0,))
        keep[0], two = product(2)
        s1[1, :, 1] = two.astype(BF16)
        for rz in early:
            first_hop(rz, (1,))
        own[0], own[1] = product(0)

    def second_hop(rz):
        for which in range(2):
            arrived(r1.at[which, rz], r1_sem.at[which, rz])
            s2[which, rz] = (keep[which, rz] + r1[which, rz, 0].astype(F32)).astype(BF16)
            go(s2.at[which, rz], r2.at[which, rz], r2_sem.at[which, rz], near[1 - which])

    def finish(rz):
        for which in range(2):
            arrived(r2.at[which, rz], r2_sem.at[which, rz])
        sides = [
            own[which, rz] + r1[which, rz, 1].astype(F32) + r2[which, rz].astype(F32) for which in range(2)
        ]
        for c in range(2):
            final[rz, c] = jnp.concatenate([one[c * 8:(c + 1) * 8] for one in sides], axis=0).astype(BF16)
        go(final.at[rz, other], back.at[plane * 2 + core], back_sem, (plane ^ rz) * group + (mine ^ 1))
        if rz:
            go(final.at[rz, core], back.at[plane * 2 + core], back_sem, across(rz))
        else:
            back[plane * 2 + core] = final[0, core]

    for g in range(CHUNKS):
        attention(g)
        for i in range(1, wave):
            leave(g, i)
        tell(g)
        if g >= 2:
            relay(g - 2, 0)

    come = range(1, wave)
    steps = []

    def then(step, *where):
        steps.append((step, *where))

    def many(step, g):
        for rz in come:
            then(step, g, rz)

    many(forward, 0)
    then(relay, 2, 0)
    many(forward, 1)
    then(relay, 3, 0)
    many(forward, 2)
    many(forward, 3)
    many(relay, 0)
    many(relay, 1)
    many(relay, 2)
    many(relay, 3)
    for g in range(CHUNKS):
        then(up, g)
    then(offer)
    then(hide)
    behind = list(range(wave - 1, -1, -1))
    then(down, behind[:WINDOW])
    for n, rz in enumerate(behind):
        then(second_hop, rz)
        if n + WINDOW < wave:
            then(first_hop, behind[n + WINDOW])
        if n >= 1:
            then(finish, behind[n - 1])
    then(finish, behind[-1])
    for step, *where in steps:
        step(*where)
    arrived(back.at[pl.ds(0, 2 * wave - 1)], back_sem)
    arrived(stream_all.at[0], pair_sem.at[2])
    high_mix = mix.astype(BF16)
    rest = mix - high_mix.astype(F32)
    middle = rest.astype(BF16)
    lowest = (rest - middle.astype(F32)).astype(BF16)
    outs = back[...].reshape(wave, 2, 16, quarter).astype(F32)
    for c in range(2):
        for which in range(2):
            rows = outs[:, c, which * 8:(which + 1) * 8].reshape(wave * 8, quarter).astype(BF16)
            added = (
                jnp.dot(lowest, rows, preferred_element_type=F32)
                + jnp.dot(middle, rows, preferred_element_type=F32)
                + jnp.dot(high_mix, rows, preferred_element_type=F32)
            )
            for g in range(CHUNKS // 2):
                at_chunk = which * (CHUNKS // 2) + g
                start = (1 + c, 3 * c)[which] * quarter + g * block
                out[:, start:start + block] = (
                    stream_all[c, at_chunk].astype(F32) + added[:, g * block:(g + 1) * block]
                ).astype(BF16)

    for r in range(1, devices // 2):
        ask(r).wait_send()

    @pl.when(core != side)
    def _():
        ask(0).wait_send()

    for copy in sends:
        copy.wait_send()


def layer(queries, keys, values, span_ids, res, gain, routes, gates, wg, wu, wd):
    devices = lax.axis_size("expert")
    group = FF_WIN // wg.shape[0]
    wave = devices // group
    tokens, width = res.shape
    half = width // 2
    hidden = wg.shape[0]
    both = 2 * tokens
    block = half // CHUNKS
    planes = SPAN // (group * tokens)
    halves = KV_HEADS // 2
    rows = wave * 16
    per_chunk = devices // 2 // CHUNKS
    hbm = pl.BlockSpec(memory_space=pl.ANY)
    dma = pltpu.SemaphoreType.DMA

    def vmem(*shape, dtype=BF16):
        return pltpu.VMEM(shape, dtype)

    scratch = {
        "keys_v": vmem(*keys.shape),
        "values_v": vmem(*values.shape),
        "ids_v": vmem(wave, 1, group * tokens, dtype=jnp.int32),
        "gain_v": vmem(1, half, dtype=F32),
        "routes_v": vmem(*routes.shape[::-1], dtype=jnp.int32),
        "gates_v": vmem(*gates.shape[::-1], dtype=F32),
        "rg_v": vmem(2, 16, 128, dtype=F32),
        "res_v": vmem(2, tokens, half),
        "w_v": vmem(2, 2, hidden, half),
        "wd_v": vmem(2, hidden, half),
        "kv_pack": vmem(KV_HEADS, tokens, 2 * HEAD_DIM),
        "kv_far": vmem(max(planes - 1, 1), KV_HEADS, tokens, 2 * HEAD_DIM),
        "kv_buf": vmem(halves, planes, group, tokens, 2 * HEAD_DIM),
        "q_buf": vmem(devices // 2, both, queries.shape[1]),
        "bias_v": vmem(SPAN, per_chunk * both, dtype=F32),
        "stream_v": vmem(CHUNKS, both, block),
        "stream_all": vmem(2, CHUNKS, tokens, block),
        "outg": vmem(CHUNKS, wave, 16, block),
        "x_buf": vmem(CHUNKS, 4, wave, 16, block),
        "pre_out": vmem(4 * rows, 4 * hidden + 128),
        "pre_in": vmem(4 * rows, 4 * hidden + 128),
        "s1": vmem(2, wave, 2, 16, half // 2),
        "r1": vmem(2, wave, 2, 16, half // 2),
        "s2": vmem(2, wave, 16, half // 2),
        "r2": vmem(2, wave, 16, half // 2),
        "keep": vmem(2, wave, 16, half // 2, dtype=F32),
        "own": vmem(2, wave, 16, half // 2, dtype=F32),
        "final": vmem(wave, 2, 16, half // 2),
        "back": vmem(2 * wave, 16, half // 2),
        "in_sem": dma((6,)),
        "w_sem": dma((2,)),
        "ready_sem": pltpu.SemaphoreType.REGULAR,
        "send_sem": dma(()),
        "ask_sem": dma(()),
        "far_sem": dma((max(planes - 1, 1), halves)),
        "kv_sem": dma((2, halves)),
        "q_sem": dma((CHUNKS,)),
        "pair_sem": dma((3,)),
        "z_sem": dma((CHUNKS, wave)),
        "x_sem": dma((CHUNKS, wave + 1)),
        "pre_sem": dma(()),
        "r1_sem": dma((2, wave)),
        "r2_sem": dma((2, wave)),
        "back_sem": dma(()),
    }
    names = ("queries", "keys", "values", "ids", "res", "gain", "routes", "gates", "wg", "wu", "wd", "out", *scratch)
    return pl.pallas_call(
        functools.partial(moe_kernel, names, group),
        out_shape=pltpu.VMEM((tokens, width), BF16),
        in_specs=[hbm] * 11,
        out_specs=pl.BlockSpec(memory_space=pltpu.VMEM),
        scratch_shapes=list(scratch.values()),
        compiler_params=pltpu.CompilerParams(
            collective_id=0, has_side_effects=True, vmem_limit_bytes=60 * 2**20
        ),
    )(
        queries, keys, values, span_ids.reshape(wave, 1, group * tokens), res, gain.reshape(1, width),
        routes.T, gates.T, wg, wu, wd,
    )


def solution(mesh):
    return jax.shard_map(
        layer,
        mesh=mesh,
        in_specs=(
            P("dp", "expert"),
            P(("dp", "expert"), None),
            P(("dp", "expert"), None),
            P("dp"),
            P(("dp", "expert"), None),
            P(),
            P(("dp", "expert"), None),
            P(("dp", "expert"), None),
            P("expert", None),
            P("expert", None),
            P("expert", None),
        ),
        out_specs=P(("dp", "expert"), None),
        check_vma=False,
    )
```

time: 52.9 us -> 46.5 us (0.88)
  Pallas kernels: 50.9 us -> 45.7 us
  local copies, waits for them, and re-layouts: 1.67 us -> 0.71 us
    pallas_call x1, Pallas kernels: 50.9 us -> 45.7 us  [layer(): pl.pallas_call(functools.partial(moe_kernel, names, group), out_shape=plt...]
    unnamed x1, local copies, waits for them, and re-layouts: 1.67 us -> 0.71 us
where the time goes in v2:
time: 46.5 us; the launch traced here: 46.4 us
  Pallas kernels  45.7 us (98%)
  local copies, waits for them, and re-layouts  0.71 us (2%)
    pallas_call x1, Pallas kernels, layer(): pl.pallas_call(functools.partial(moe_kernel, names, group), out_shape=plt...  45.7 us

profile of v2, /device:TPU:0, one launch (start us, length us, event | category | flops | bytes accessed | tf_op | source)
XLA Modules:
  0.0 46.4 jit_solution(15863668508121744317)
XLA Ops:
  0.0 45.7 %shard_map.109 = bf16[32,4096]{1,0:T(8,128)(2,1)S(1)} custom-call(bf16[1024,128]{1,0:T(8,128)(2,1)} %refs_0_.1, bf16[32,256]{1,0:T(8,128)(2,1)} %refs_1_.1, bf16[32,256]{1,0:T(8,128)(2,1)} %refs_2_.1, s32[4,1,256]{2,1,0:T(1,128)} %bitcast.5, bf16[32,4096]{1,0:T(8,128)(2,1)} %refs_4_.1, f32[1,4096]{1,0:T(1,128)} %bitcast.4, s32[8,32]{1,0:T(8,128)} %bitcast.6, ...), custom_call_target="tpu_custom_call" | custom-call | tf_op jit(solution)/shard_map/pallas_call | solution.py:518
  45.7 0.7 %copy.13 = bf16[32,4096]{1,0:T(8,128)(2,1)} copy(bf16[32,4096]{1,0:T(8,128)(2,1)S(1)} %shard_map.109) | data formatting | bytes 524288

commit v3 on v2

--- a/solution.py
+++ b/solution.py
@@ -14,6 +14,7 @@
 SPAN = 512
 CHUNKS = 4
 WINDOW = 3
+SOON = (1,)
 MESH = pl.DeviceIdType.MESH
 F32 = jnp.float32
 BF16 = jnp.bfloat16
@@ -164,22 +165,32 @@
         source = queries.at[pl.ds(pl.multiple_of(pair * both, both), both)]
         return remote(source, q_buf.at[number], at["ask_sem"], query_sem, pair * 2 + side)
 
-    def ask_all():
-        for r in range(devices // 2 - 1, 0, -1):
-            ask(r).start()
-
-        @pl.when(core == side)
-        def _():
-            source = queries.at[pl.ds(pl.multiple_of(me // 2 * both, both), both)]
-            pltpu.make_async_copy(source, q_buf.at[number], query_sem).start()
-
-        @pl.when(core != side)
-        def _():
-            ask(0).start()
+    def ask_planes(distances):
+        for rz in distances:
+            for r in range((rz + 1) * group // 2 - 1, rz * group // 2 - 1, -1):
+                if r:
+                    ask(r).start()
+        if 0 in distances:
+
+            @pl.when(core == side)
+            def _():
+                source = queries.at[pl.ds(pl.multiple_of(me // 2 * both, both), both)]
+                pltpu.make_async_copy(source, q_buf.at[number], query_sem).start()
+
+            @pl.when(core != side)
+            def _():
+                ask(0).start()
+
+    distant = list(range(wave - 1, -1, -1))
+    soon = SOON
 
     @pl.when(number < devices // 4)
     def _():
-        ask_all()
+        ask_planes(distant)
+
+    @pl.when(number >= devices // 4)
+    def _():
+        ask_planes([rz for rz in distant if rz in soon])
 
     for name in ("routes", "gates"):
         fetched[name].wait()
@@ -220,7 +231,7 @@
 
     @pl.when(number >= devices // 4)
     def _():
-        ask_all()
+        ask_planes([rz for rz in distant if rz not in soon])
 
     def gathered(h):
         arrived(kv_buf.at[h, 0, pl.ds(0, group - 1)], kv_sem.at[0, h])
@@ -236,16 +247,16 @@
         head = g * halves // CHUNKS
         held = kv_buf[head].reshape(SPAN, 2 * HEAD_DIM)
         key_blk = held[:, :HEAD_DIM]
-        value_rows = held.T[HEAD_DIM:]
+        value_rows = jnp.concatenate([held.T[HEAD_DIM:], jnp.ones((16, SPAN), BF16)], axis=0)
         query = q_buf[g * per_chunk:(g + 1) * per_chunk].reshape(wide, -1) * BF16(1.0 / math.sqrt(HEAD_DIM))
-        heads = []
-        for number in range(query.shape[1] // HEAD_DIM):
-            one = query[:, number * HEAD_DIM:(number + 1) * HEAD_DIM]
-            scores = lax.dot_general(key_blk, one, (((1,), (1,)), ((), ())), preferred_element_type=F32)
-            scores = scores + bias_v[...]
-            raised = jnp.exp(scores - jnp.max(scores, axis=0, keepdims=True))
-            total = jnp.sum(raised, axis=0, keepdims=True)
-            heads.append(jnp.dot(value_rows, raised.astype(BF16), preferred_element_type=F32) * (1.0 / total))
+        count = query.shape[1] // HEAD_DIM
+        query = jnp.concatenate([query[:, n * HEAD_DIM:(n + 1) * HEAD_DIM] for n in range(count)], axis=0)
+        scores = lax.dot_general(key_blk, query, (((1,), (1,)), ((), ())), preferred_element_type=F32)
+        scores = scores + jnp.concatenate([bias_v[...]] * count, axis=1)
+        raised = jnp.exp(scores - jnp.max(scores, axis=0, keepdims=True)).astype(BF16)
+        summed = jnp.dot(value_rows, raised, preferred_element_type=F32)
+        summed = summed[:HEAD_DIM] * (1.0 / summed[HEAD_DIM:HEAD_DIM + 1])
+        heads = [summed[:, n * wide:(n + 1) * wide] for n in range(count)]
         joined = heads[0] if len(heads) == 1 else jnp.concatenate(heads, axis=0)
         joined = joined.T.astype(BF16)
         return jnp.concatenate([joined[i * both:(i + 1) * both] for i in range(per_chunk)], axis=1)

time: 46.5 us -> 45.8 us (0.985)
  Pallas kernels: 45.7 us -> 44.9 us
    pallas_call x1, Pallas kernels: 45.7 us -> 44.9 us  [layer(): pl.pallas_call(functools.partial(moe_kernel, names, group), out_shape=plt...]
where the time goes in v3:
time: 45.8 us; the launch traced here: 45.7 us
  Pallas kernels  44.9 us (98%)
  local copies, waits for them, and re-layouts  0.71 us (2%)
    pallas_call x1, Pallas kernels, layer(): pl.pallas_call(functools.partial(moe_kernel, names, group), out_shape=plt...  44.9 us

profile of v3, /device:TPU:0, one launch (start us, length us, event | category | flops | bytes accessed | tf_op | source)
XLA Modules:
  0.0 45.7 jit_solution(4943626325541918301)
XLA Ops:
  0.0 44.9 %shard_map.109 = bf16[32,4096]{1,0:T(8,128)(2,1)S(1)} custom-call(bf16[1024,128]{1,0:T(8,128)(2,1)} %refs_0_.1, bf16[32,256]{1,0:T(8,128)(2,1)} %refs_1_.1, bf16[32,256]{1,0:T(8,128)(2,1)} %refs_2_.1, s32[4,1,256]{2,1,0:T(1,128)} %bitcast.5, bf16[32,4096]{1,0:T(8,128)(2,1)} %refs_4_.1, f32[1,4096]{1,0:T(1,128)} %bitcast.4, s32[8,32]{1,0:T(8,128)} %bitcast.6, ...), custom_call_target="tpu_custom_call" | custom-call | tf_op jit(solution)/shard_map/pallas_call | solution.py:529
  44.9 0.7 %copy.13 = bf16[32,4096]{1,0:T(8,128)(2,1)} copy(bf16[32,4096]{1,0:T(8,128)(2,1)S(1)} %shard_map.109) | data formatting | bytes 524288

commit v4 on v3

--- a/solution.py
+++ b/solution.py
@@ -276,7 +276,7 @@
         outg[g] = jnp.dot(chosen, stream, preferred_element_type=F32).astype(BF16).reshape(wave, 16, block)
 
     def leave(g, rz):
-        go(outg.at[g, plane ^ rz], x_buf.at[g, 0, rz], z_sem.at[g, rz], across(rz))
+        go(outg.at[g, plane ^ rz], x_buf.at[g, 0, rz], z_sem.at[g, rz - 1], across(rz))
 
     def spread(g, rz):
         for hop in range(2):
@@ -284,7 +284,7 @@
             go(x_buf.at[g, 0, rz], x_buf.at[g, 1 + hop, rz], recv, near[hop])
 
     def forward(g, rz):
-        arrived(x_buf.at[g, 0, rz], z_sem.at[g, rz])
+        arrived(x_buf.at[g, 0, rz], z_sem.at[g, rz - 1])
         spread(g, rz)
 
     def relay(g, rz):
@@ -341,38 +341,32 @@
         total["hidden"] = (gate_pre / (1.0 + jnp.exp(-gate_pre)) * up_pre).astype(BF16)
         arrived(wd_v, w_sem.at[1])
 
-    def product(blk):
-        weight = wd_v[...].reshape(-1, half)
-        piece = jnp.dot(total["hidden"][blk * rows:(blk + 1) * rows], weight, preferred_element_type=F32)
-        piece = piece.reshape(wave, 16, half)
-        return piece[:, :, :quarter], piece[:, :, quarter:]
+    def product(blks, which):
+        hidden = jnp.concatenate([total["hidden"][blk * rows:(blk + 1) * rows] for blk in blks], axis=0)
+        weight = wd_v[:, :, which * quarter:(which + 1) * quarter].reshape(-1, quarter)
+        return jnp.dot(hidden, weight, preferred_element_type=F32).reshape(2, wave, 16, quarter)
 
     def first_hop(rz, sides=(0, 1)):
         for which in sides:
             go(s1.at[which, rz], r1.at[which, rz], r1_sem.at[which, rz], near[which])
 
     def down(early):
-        one, two = product(3)
-        s1[0, :, 0], s1[1, :, 0] = one.astype(BF16), two.astype(BF16)
-        one, keep[1] = product(1)
-        s1[0, :, 1] = one.astype(BF16)
-        for rz in early:
-            first_hop(rz, (0,))
-        keep[0], two = product(2)
-        s1[1, :, 1] = two.astype(BF16)
-        for rz in early:
-            first_hop(rz, (1,))
-        own[0], own[1] = product(0)
+        for which in range(2):
+            piece = product((3, 1 + which), which).astype(BF16)
+            s1[which, :, 0], s1[which, :, 1] = piece[0], piece[1]
+            for rz in early:
+                first_hop(rz, (which,))
+        for which in range(2):
+            keep[which], own[which] = product((2 - which, 0), which)
 
     def second_hop(rz):
         for which in range(2):
             arrived(r1.at[which, rz], r1_sem.at[which, rz])
             s2[which, rz] = (keep[which, rz] + r1[which, rz, 0].astype(F32)).astype(BF16)
-            go(s2.at[which, rz], r2.at[which, rz], r2_sem.at[which, rz], near[1 - which])
+            go(s2.at[which, rz], r2.at[which, rz], r2_sem.at[rz], near[1 - which])
 
     def finish(rz):
-        for which in range(2):
-            arrived(r2.at[which, rz], r2_sem.at[which, rz])
+        arrived(r2.at[:, rz], r2_sem.at[rz])
         sides = [
             own[which, rz] + r1[which, rz, 1].astype(F32) + r2[which, rz].astype(F32) for which in range(2)
         ]
@@ -518,11 +512,11 @@
         "kv_sem": dma((2, halves)),
         "q_sem": dma((CHUNKS,)),
         "pair_sem": dma((3,)),
-        "z_sem": dma((CHUNKS, wave)),
+        "z_sem": dma((CHUNKS, wave - 1)),
         "x_sem": dma((CHUNKS, wave + 1)),
         "pre_sem": dma(()),
         "r1_sem": dma((2, wave)),
-        "r2_sem": dma((2, wave)),
+        "r2_sem": dma((wave,)),
         "back_sem": dma(()),
     }
     names = ("queries", "keys", "values", "ids", "res", "gain", "routes", "gates", "wg", "wu", "wd", "out", *scratch)

time: 45.8 us -> 45.5 us (level)
  no operation moved by 1% of the time
where the time goes in v4:
time: 45.5 us; the launch traced here: 45.3 us
  Pallas kernels  44.6 us (98%)
  local copies, waits for them, and re-layouts  0.71 us (2%)
    pallas_call x1, Pallas kernels, layer(): pl.pallas_call(functools.partial(moe_kernel, names, group), out_shape=plt...  44.6 us

profile of v4, /device:TPU:0, one launch (start us, length us, event | category | flops | bytes accessed | tf_op | source)
XLA Modules:
  0.0 45.3 jit_solution(14470986713569235152)
XLA Ops:
  0.0 44.6 %shard_map.109 = bf16[32,4096]{1,0:T(8,128)(2,1)S(1)} custom-call(bf16[1024,128]{1,0:T(8,128)(2,1)} %refs_0_.1, bf16[32,256]{1,0:T(8,128)(2,1)} %refs_1_.1, bf16[32,256]{1,0:T(8,128)(2,1)} %refs_2_.1, s32[4,1,256]{2,1,0:T(1,128)} %bitcast.5, bf16[32,4096]{1,0:T(8,128)(2,1)} %refs_4_.1, f32[1,4096]{1,0:T(1,128)} %bitcast.4, s32[8,32]{1,0:T(8,128)} %bitcast.6, ...), custom_call_target="tpu_custom_call" | custom-call | tf_op jit(solution)/shard_map/pallas_call | solution.py:523
  44.6 0.7 %copy.13 = bf16[32,4096]{1,0:T(8,128)(2,1)} copy(bf16[32,4096]{1,0:T(8,128)(2,1)S(1)} %shard_map.109) | data formatting | bytes 524288

commit v5 on v4

--- a/solution.py
+++ b/solution.py
@@ -186,7 +186,7 @@
 
     @pl.when(number < devices // 4)
     def _():
-        ask_planes(distant)
+        ask_planes(distant[:-1])
 
     @pl.when(number >= devices // 4)
     def _():
@@ -203,6 +203,11 @@
             share(h, kv_far.at[rz - 1], (plane ^ rz) % planes, kv_sem.at[1, h])
 
     pass_on(0)
+
+    @pl.when(number < devices // 4)
+    def _():
+        ask_planes([0])
+
     split(res, res_v.at[core], pair_sem.at[1], partner)
     fetched["ids"].wait()
     _, mix = route_matrix(routes_v[...].astype(F32).T, gates_v[...].T, wave, 8, 1)

time: 45.5 us -> 45.4 us (level)
  no operation moved by 1% of the time
where the time goes in v5:
time: 45.4 us; the launch traced here: 45.3 us
  Pallas kernels  44.6 us (98%)
  local copies, waits for them, and re-layouts  0.71 us (2%)
    pallas_call x1, Pallas kernels, layer(): pl.pallas_call(functools.partial(moe_kernel, names, group), out_shape=plt...  44.6 us

profile of v5, /device:TPU:0, one launch (start us, length us, event | category | flops | bytes accessed | tf_op | source)
XLA Modules:
  0.0 45.3 jit_solution(10821056365382305846)
XLA Ops:
  0.0 44.6 %shard_map.109 = bf16[32,4096]{1,0:T(8,128)(2,1)S(1)} custom-call(bf16[1024,128]{1,0:T(8,128)(2,1)} %refs_0_.1, bf16[32,256]{1,0:T(8,128)(2,1)} %refs_1_.1, bf16[32,256]{1,0:T(8,128)(2,1)} %refs_2_.1, s32[4,1,256]{2,1,0:T(1,128)} %bitcast.5, bf16[32,4096]{1,0:T(8,128)(2,1)} %refs_4_.1, f32[1,4096]{1,0:T(1,128)} %bitcast.4, s32[8,32]{1,0:T(8,128)} %bitcast.6, ...), custom_call_target="tpu_custom_call" | custom-call | tf_op jit(solution)/shard_map/pallas_call | solution.py:528
  44.6 0.7 %copy.13 = bf16[32,4096]{1,0:T(8,128)(2,1)} copy(bf16[32,4096]{1,0:T(8,128)(2,1)S(1)} %shard_map.109) | data formatting | bytes 524288

commit v6 on v5

--- a/solution.py
+++ b/solution.py
@@ -13,7 +13,10 @@
 FF_WIN = 1024
 SPAN = 512
 CHUNKS = 4
-WINDOW = 3
+WINDOW = 5
+AHEAD = 3
+NEXT = 2
+LAG = 2
 SOON = (1,)
 MESH = pl.DeviceIdType.MESH
 F32 = jnp.float32
@@ -351,26 +354,28 @@
         weight = wd_v[:, :, which * quarter:(which + 1) * quarter].reshape(-1, quarter)
         return jnp.dot(hidden, weight, preferred_element_type=F32).reshape(2, wave, 16, quarter)
 
-    def first_hop(rz, sides=(0, 1)):
+    def first_hop(kind, rz, sides=(0, 1)):
         for which in sides:
-            go(s1.at[which, rz], r1.at[which, rz], r1_sem.at[which, rz], near[which])
+            go(s1.at[which, rz, kind], r1.at[which, rz, kind], r1_sem.at[which, rz, kind], near[which])
 
     def down(early):
         for which in range(2):
             piece = product((3, 1 + which), which).astype(BF16)
             s1[which, :, 0], s1[which, :, 1] = piece[0], piece[1]
-            for rz in early:
-                first_hop(rz, (which,))
+            for kind, rz in early:
+                first_hop(kind, rz, (which,))
         for which in range(2):
             keep[which], own[which] = product((2 - which, 0), which)
 
     def second_hop(rz):
         for which in range(2):
-            arrived(r1.at[which, rz], r1_sem.at[which, rz])
+            arrived(r1.at[which, rz, 0], r1_sem.at[which, rz, 0])
             s2[which, rz] = (keep[which, rz] + r1[which, rz, 0].astype(F32)).astype(BF16)
             go(s2.at[which, rz], r2.at[which, rz], r2_sem.at[rz], near[1 - which])
 
     def finish(rz):
+        for which in range(2):
+            arrived(r1.at[which, rz, 1], r1_sem.at[which, rz, 1])
         arrived(r2.at[:, rz], r2_sem.at[rz])
         sides = [
             own[which, rz] + r1[which, rz, 1].astype(F32) + r2[which, rz].astype(F32) for which in range(2)
@@ -416,14 +421,22 @@
     then(offer)
     then(hide)
     behind = list(range(wave - 1, -1, -1))
-    then(down, behind[:WINDOW])
+    pieces = [(0, rz) for rz in behind[:AHEAD]]
+    for n, rz in enumerate(behind):
+        pieces.append((1, rz))
+        if n + AHEAD < wave:
+            pieces.append((0, behind[n + AHEAD]))
+    then(down, pieces[:WINDOW])
+    del pieces[:WINDOW]
     for n, rz in enumerate(behind):
         then(second_hop, rz)
-        if n + WINDOW < wave:
-            then(first_hop, behind[n + WINDOW])
-        if n >= 1:
-            then(finish, behind[n - 1])
-    then(finish, behind[-1])
+        for kind, late in pieces[:NEXT]:
+            then(first_hop, kind, late)
+        del pieces[:NEXT]
+        if n >= LAG:
+            then(finish, behind[n - LAG])
+    for rz in behind[-LAG:]:
+        then(finish, rz)
     for step, *where in steps:
         step(*where)
     arrived(back.at[pl.ds(0, 2 * wave - 1)], back_sem)
@@ -520,7 +533,7 @@
         "z_sem": dma((CHUNKS, wave - 1)),
         "x_sem": dma((CHUNKS, wave + 1)),
         "pre_sem": dma(()),
-        "r1_sem": dma((2, wave)),
+        "r1_sem": dma((2, wave, 2)),
         "r2_sem": dma((wave,)),
         "back_sem": dma(()),
     }

time: 45.4 us -> 45.1 us (level)
  no operation moved by 1% of the time
where the time goes in v6:
time: 45.1 us; the launch traced here: 45 us
  Pallas kernels  44.2 us (98%)
  local copies, waits for them, and re-layouts  0.71 us (2%)
    pallas_call x1, Pallas kernels, layer(): pl.pallas_call(functools.partial(moe_kernel, names, group), out_shape=plt...  44.2 us

profile of v6, /device:TPU:0, one launch (start us, length us, event | category | flops | bytes accessed | tf_op | source)
XLA Modules:
  0.0 45.0 jit_solution(13739011540830766010)
XLA Ops:
  0.0 44.2 %shard_map.109 = bf16[32,4096]{1,0:T(8,128)(2,1)S(1)} custom-call(bf16[1024,128]{1,0:T(8,128)(2,1)} %refs_0_.1, bf16[32,256]{1,0:T(8,128)(2,1)} %refs_1_.1, bf16[32,256]{1,0:T(8,128)(2,1)} %refs_2_.1, s32[4,1,256]{2,1,0:T(1,128)} %bitcast.5, bf16[32,4096]{1,0:T(8,128)(2,1)} %refs_4_.1, f32[1,4096]{1,0:T(1,128)} %bitcast.4, s32[8,32]{1,0:T(8,128)} %bitcast.6, ...), custom_call_target="tpu_custom_call" | custom-call | tf_op jit(solution)/shard_map/pallas_call | solution.py:541
  44.2 0.7 %copy.13 = bf16[32,4096]{1,0:T(8,128)(2,1)} copy(bf16[32,4096]{1,0:T(8,128)(2,1)S(1)} %shard_map.109) | data formatting | bytes 524288

commit v7 on v6

--- a/solution.py
+++ b/solution.py
@@ -390,9 +390,9 @@
 
     for g in range(CHUNKS):
         attention(g)
+        tell(g)
         for i in range(1, wave):
             leave(g, i)
-        tell(g)
         if g >= 2:
             relay(g - 2, 0)
 

time: 45.1 us -> 45.1 us (level)
  no operation moved by 1% of the time
where the time goes in v7:
time: 45.1 us; the launch traced here: 45 us
  Pallas kernels  44.2 us (98%)
  local copies, waits for them, and re-layouts  0.71 us (2%)
    pallas_call x1, Pallas kernels, layer(): pl.pallas_call(functools.partial(moe_kernel, names, group), out_shape=plt...  44.2 us

profile of v7, /device:TPU:0, one launch (start us, length us, event | category | flops | bytes accessed | tf_op | source)
XLA Modules:
  0.0 45.0 jit_solution(10344476219804891641)
XLA Ops:
  0.0 44.2 %shard_map.109 = bf16[32,4096]{1,0:T(8,128)(2,1)S(1)} custom-call(bf16[1024,128]{1,0:T(8,128)(2,1)} %refs_0_.1, bf16[32,256]{1,0:T(8,128)(2,1)} %refs_1_.1, bf16[32,256]{1,0:T(8,128)(2,1)} %refs_2_.1, s32[4,1,256]{2,1,0:T(1,128)} %bitcast.5, bf16[32,4096]{1,0:T(8,128)(2,1)} %refs_4_.1, f32[1,4096]{1,0:T(1,128)} %bitcast.4, s32[8,32]{1,0:T(8,128)} %bitcast.6, ...), custom_call_target="tpu_custom_call" | custom-call | tf_op jit(solution)/shard_map/pallas_call | solution.py:541
  44.3 0.7 %copy.13 = bf16[32,4096]{1,0:T(8,128)(2,1)} copy(bf16[32,4096]{1,0:T(8,128)(2,1)S(1)} %shard_map.109) | data formatting | bytes 524288

commit v8 on v7

--- a/solution.py
+++ b/solution.py
@@ -406,16 +406,12 @@
         for rz in come:
             then(step, g, rz)
 
-    many(forward, 0)
+    for g in range(CHUNKS):
+        many(forward, g)
     then(relay, 2, 0)
-    many(forward, 1)
     then(relay, 3, 0)
-    many(forward, 2)
-    many(forward, 3)
-    many(relay, 0)
-    many(relay, 1)
-    many(relay, 2)
-    many(relay, 3)
+    for g in range(CHUNKS):
+        many(relay, g)
     for g in range(CHUNKS):
         then(up, g)
     then(offer)

time: 45.1 us -> 45.2 us (level)
  no operation moved by 1% of the time
where the time goes in v8:
time: 45.2 us; the launch traced here: 45.1 us
  Pallas kernels  44.3 us (98%)
  local copies, waits for them, and re-layouts  0.71 us (2%)
    pallas_call x1, Pallas kernels, layer(): pl.pallas_call(functools.partial(moe_kernel, names, group), out_shape=plt...  44.3 us

profile of v8, /device:TPU:0, one launch (start us, length us, event | category | flops | bytes accessed | tf_op | source)
XLA Modules:
  0.0 45.1 jit_solution(9043342729206534769)
XLA Ops:
  0.0 44.3 %shard_map.109 = bf16[32,4096]{1,0:T(8,128)(2,1)S(1)} custom-call(bf16[1024,128]{1,0:T(8,128)(2,1)} %refs_0_.1, bf16[32,256]{1,0:T(8,128)(2,1)} %refs_1_.1, bf16[32,256]{1,0:T(8,128)(2,1)} %refs_2_.1, s32[4,1,256]{2,1,0:T(1,128)} %bitcast.5, bf16[32,4096]{1,0:T(8,128)(2,1)} %refs_4_.1, f32[1,4096]{1,0:T(1,128)} %bitcast.4, s32[8,32]{1,0:T(8,128)} %bitcast.6, ...), custom_call_target="tpu_custom_call" | custom-call | tf_op jit(solution)/shard_map/pallas_call | solution.py:537
  44.4 0.7 %copy.13 = bf16[32,4096]{1,0:T(8,128)(2,1)} copy(bf16[32,4096]{1,0:T(8,128)(2,1)S(1)} %shard_map.109) | data formatting | bytes 524288
